TPU v7x, 512 devices: a whole 4x8x8 slice. The times are simulated.
512 devices in a mesh: row: 16 (over y, core), col: 8 (over z), depth: 4 (over x).
Axes of the slice: x: 4, y: 8, z: 8, core: 2. Of those that a mesh axis runs over, the one named last changes fastest.
Arguments:
- density: float32 [512, 5, 128, 128], P(('row', 'depth'), None, 'col'), may hold values from -0.6 to 0.6
- pattern: int32 [512, 5], P(('row', 'depth')), may hold values 0 or 1
Outputs:
- purified: float32 [512, 5, 128, 128], P(('row', 'depth'), None, 'col')
All inputs are finite; a program needn't handle non-finite values. No bound on the sum of `pattern` on one device may be relied on, other than what follows from the above.
Results may differ from a plain program's by a relative error of at most 0.0001.
Values sent between devices are 32-bit elements; how exact they have to be, the bound alone decides.
No kernel may reach another device: no remote copies, remote signals or barrier semaphores. Data moves between devices by JAX's collectives and lax.ppermute only.
A program may use at most 64 MiB of HBM per device.

v0:
```python
import jax
import jax.numpy as jnp
from jax import lax
from jax.sharding import PartitionSpec as P

HALF = 2
WIDE = 5


def with_halo(cells, sides, width):
    for axis, dim in sides:
        count = lax.axis_size(axis)
        head = lax.slice_in_dim(cells, 0, width, axis=dim)
        tail = lax.slice_in_dim(cells, cells.shape[dim] - width, cells.shape[dim], axis=dim)
        cells = jnp.concatenate(
            [
                lax.ppermute(tail, axis, [(i, (i + 1) % count) for i in range(count)]),
                cells,
                lax.ppermute(head, axis, [((i + 1) % count, i) for i in range(count)]),
            ],
            axis=dim,
        )
    return cells


def banded_local(left_tiles, extended, pattern):
    rows_here = left_tiles.shape[0]
    summed = jnp.zeros(left_tiles.shape, jnp.float32)
    for source in range(WIDE):
        first_slot = max(0, source - HALF)
        last_slot = min(WIDE, source + HALF + 1)
        partner = extended[
            source : source + rows_here, first_slot - source + HALF : last_slot - source + HALF
        ]
        contrib = jnp.einsum(
            "iab,itbc->itac", left_tiles[:, source], partner, precision=lax.Precision.HIGHEST
        )
        summed = summed.at[:, first_slot:last_slot].add(contrib)
    return summed * pattern[:, :, None, None].astype(jnp.float32)


def shards(density, pattern):
    masked = density * pattern[:, :, None, None].astype(jnp.float32)
    whole_tiles = lax.all_gather(masked, "col", axis=2, tiled=True)
    extended = with_halo(whole_tiles, ((("row", "depth"), 0),), HALF)
    square = banded_local(masked, extended, pattern)
    cube = banded_local(square, extended, pattern)
    return 3.0 * square - 2.0 * cube


def solution(mesh):
    in_specs = (P(("row", "depth"), None, "col", None), P(("row", "depth"), None))
    out_specs = P(("row", "depth"), None, "col", None)
    return jax.shard_map(shards, mesh=mesh, in_specs=in_specs, out_specs=out_specs, check_vma=False)
```

profile of v0, /device:TPU:1, one launch (start us, length us, event | category | flops | bytes accessed | tf_op | source)
XLA Modules:
  0.0 108.2 jit_solution(13460640927756689920)
XLA Ops:
  6.5 0.0 all-gather.2.cloned.1.call-start
  6.5 0.7 convert_element_type.6
  7.2 0.1 copy.3
  7.3 1.8 %copy_multiply_fusion = f32[8,5,16,128]{3,2,0,1:T(8,128)} fusion(f32[8,5,16,128]{3,2,1,0:T(8,128)} %param.26, f32[8,5]{0,1:T(8,128)S(1)} %copy.3), kind=kLoop, calls=%fused_computation.18 | loop fusion | flops 81920 | bytes 655520 | tf_op jit(solution)/shard_map/mul | solution.py:43
  9.1 0.0 all-gather.2.cloned.1.call-update
  9.1 48.3 %all-gather.2.cloned.1.call-done = f32[8,5,128,128]{3,2,0,1:T(8,128)} async-done(((f32[8,5,16,128]{3,2,0,1:T(8,128)}), f32[8,5,128,128]{3,2,0,1:T(8,128)}) %all-gather.2.cloned.1.call-update) | async-done | bytes 2621456 | tf_op jit(solution)/shard_map/all_gather | solution.py:44
  57.5 0.0 copy-start
  57.5 1.5 %fusion.10 = (f32[2,5,128,128]{3,2,0,1:T(8,128)S(1)}, f32[2,5,128,128]{3,2,0,1:T(8,128)S(1)}) fusion(f32[8,5,128,128]{3,2,0,1:T(8,128)} %all-gather.2.cloned.1.call-done), kind=kLoop, calls=%fused_computation.41 | loop fusion | bytes 2621440 | tf_op jit(solution)/shard_map/slice | solution.py:13
  59.0 3.1 %collective-permute-start = (f32[2,5,128,128]{3,2,0,1:T(8,128)S(1)}, f32[2,5,128,128]{3,2,0,1:T(8,128)S(1)}, u32[]{:S(2)}, u32[]{:S(2)}) collective-permute-start(f32[2,5,128,128]{3,2,0,1:T(8,128)S(1)} %get-tuple-element.142), channel_id=1, source_target_pairs={{0,1},{1,2},{2,3},{3,32},{32,33},{33,34},{34,35},{35,64},{64,65},{... | collective-permute-start | bytes 1966088 | tf_op jit(solution)/shard_map/ppermute | solution.py:17
  62.1 6.9 %collective-permute-start.1 = (f32[2,5,128,128]{3,2,0,1:T(8,128)S(1)}, f32[2,5,128,128]{3,2,0,1:T(8,128)S(1)}, u32[]{:S(2)}, u32[]{:S(2)}) collective-permute-start(f32[2,5,128,128]{3,2,0,1:T(8,128)S(1)} %get-tuple-element.141), channel_id=1, source_target_pairs={{1,0},{2,1},{3,2},{32,3},{33,32},{34,33},{35,34},{64,35},{65,64},{... | collective-permute-start | bytes 1966088 | tf_op jit(solution)/shard_map/ppermute | solution.py:19
  69.1 13.3 %collective-permute-done = f32[2,5,128,128]{3,2,0,1:T(8,128)S(1)} collective-permute-done((f32[2,5,128,128]{3,2,0,1:T(8,128)S(1)}, f32[2,5,128,128]{3,2,0,1:T(8,128)S(1)}, u32[]{:S(2)}, u32[]{:S(2)}) %collective-permute-start) | collective-permute-done | bytes 655392 | tf_op jit(solution)/shard_map/ppermute | solution.py:17
  82.5 0.0 copy-done
  82.5 0.0 copy-start.1
  82.5 0.6 constant_dynamic-update-slice_fusion.3
  83.1 0.3 copy-done.1
  83.5 1.4 %convolution_bitcast_fusion.9 = f32[8,3,16,128]{3,2,0,1:T(8,128)S(1)} fusion(f32[10,5,128,128]{3,2,0,1:T(8,128)S(1)} %get-tuple-element.144, f32[8,5,16,128]{3,2,0,1:T(8,128)S(1)} %copy-done.1), kind=kOutput, calls=%fused_computation.17 | convolution fusion | flops 75497472 | bytes 3538944 | tf_op jit(solution)/shard_map/iab,itbc->itac/dot_general | solution.py:35
  84.9 1.9 %fusion.7 = f32[8,5,16,128]{3,2,0,1:T(8,128)S(1)} fusion(f32[8,5,16,128]{3,2,0,1:T(8,128)S(1)} %scatter-add.26, f32[10,5,128,128]{3,2,0,1:T(8,128)S(1)} %get-tuple-element.144, f32[8,5,16,128]{3,2,0,1:T(8,128)S(1)} %copy-done.1), kind=kOutput, calls=%fused_computation.13 | convolution fusion | flops 100728832 | bytes 3866624 | tf_op jit(solution)/shard_map/iab,itbc->itac/dot_general | solution.py:35
  86.8 1.7 %fusion.1 = f32[8,5,16,128]{3,2,0,1:T(8,128)S(1)} fusion(f32[8,5,16,128]{3,2,0,1:T(8,128)S(1)} %fusion.7, f32[8,5,128,128]{3,2,0,1:T(8,128)S(1)} %copy-done, f32[8,5,16,128]{3,2,0,1:T(8,128)S(1)} %copy-done.1), kind=kOutput, calls=%fused_computation.3 | convolution fusion | flops 125911040 | bytes 3342336 | tf_op jit(solution)/shard_map/iab,itbc->itac/dot_general | solution.py:35
  88.4 0.0 collective-permute-done.1
  88.5 1.9 %fusion.5 = f32[8,4,16,128]{3,2,0,1:T(8,128)S(1)} fusion(f32[10,5,128,128]{3,2,0,1:T(8,128)S(1)} %constant_dynamic-update-slice_fusion.2, f32[8,5,16,128]{3,2,0,1:T(8,128)S(1)} %fusion.1, f32[8,5,16,128]{3,2,0,1:T(8,128)S(1)} %copy-done.1), kind=kOutput, calls=%fused_computation.10 | convolution fusion | flops 100728832 | bytes 3866624 | tf_op jit(solution)/shard_map/iab,itbc->itac/dot_general | solution.py:35
  90.4 1.4 %fusion.9 = f32[8,5,16,128]{3,2,0,1:T(8,128)S(1)} fusion(f32[8,5,16,128]{3,2,0,1:T(8,128)S(1)} %constant_dynamic-update-slice_fusion.5, f32[8,4,16,128]{3,2,0,1:T(8,128)S(1)} %fusion.5, f32[10,5,128,128]{3,2,0,1:T(8,128)S(1)} %constant_dynamic-update-slice_fusion.2, f32[8,5,16,128]{3,2,0,1:T(8,128)S(1)} %copy-done.1), kind=kOutput, calls=%fused_computation.23 | convolution fusion | flops 75546624 | bytes 3735552 | tf_op jit(solution)/shard_map/iab,itbc->itac/dot_general | solution.py:35
  91.8 0.1 broadcast_multiply_fusion
  92.0 1.4 %convolution_bitcast_fusion.7 = f32[8,3,16,128]{3,2,0,1:T(8,128)S(1)} fusion(f32[10,5,128,128]{3,2,0,1:T(8,128)S(1)} %get-tuple-element.144, f32[8,5,16,128]{3,2,0,1:T(8,128)S(1)} %broadcast_multiply_fusion), kind=kOutput, calls=%fused_computation.15 | convolution fusion | flops 75497472 | bytes 3538944 | tf_op jit(solution)/shard_map/iab,itbc->itac/dot_general | solution.py:35
  93.4 1.9 %fusion.4 = f32[8,5,16,128]{3,2,0,1:T(8,128)S(1)} fusion(f32[8,5,16,128]{3,2,0,1:T(8,128)S(1)} %scatter-add.34, f32[10,5,128,128]{3,2,0,1:T(8,128)S(1)} %get-tuple-element.144, f32[8,5,16,128]{3,2,0,1:T(8,128)S(1)} %broadcast_multiply_fusion), kind=kOutput, calls=%fused_computation.8 | convolution fusion | flops 100728832 | bytes 3866624 | tf_op jit(solution)/shard_map/iab,itbc->itac/dot_general | solution.py:35
  95.3 1.8 %fusion = f32[8,5,16,128]{3,2,0,1:T(8,128)S(1)} fusion(f32[8,5,16,128]{3,2,0,1:T(8,128)S(1)} %fusion.4, f32[8,5,128,128]{3,2,0,1:T(8,128)S(1)} %copy-done, f32[8,5,16,128]{3,2,0,1:T(8,128)S(1)} %broadcast_multiply_fusion), kind=kOutput, calls=%fused_computation.1 | convolution fusion | flops 125911040 | bytes 3342336 | tf_op jit(solution)/shard_map/iab,itbc->itac/dot_general | solution.py:35
  97.1 1.9 %fusion.2 = f32[8,4,16,128]{3,2,0,1:T(8,128)S(1)} fusion(f32[10,5,128,128]{3,2,0,1:T(8,128)S(1)} %constant_dynamic-update-slice_fusion.2, f32[8,5,16,128]{3,2,0,1:T(8,128)S(1)} %fusion, f32[8,5,16,128]{3,2,0,1:T(8,128)S(1)} %broadcast_multiply_fusion), kind=kOutput, calls=%fused_computation.5 | convolution fusion | flops 100728832 | bytes 3866624 | tf_op jit(solution)/shard_map/iab,itbc->itac/dot_general | solution.py:35
  99.0 1.4 %fusion.8 = f32[8,5,16,128]{3,2,0,1:T(8,128)S(1)} fusion(f32[8,5,16,128]{3,2,0,1:T(8,128)S(1)} %constant_dynamic-update-slice_fusion.4, f32[8,4,16,128]{3,2,0,1:T(8,128)S(1)} %fusion.2, f32[10,5,128,128]{3,2,0,1:T(8,128)S(1)} %constant_dynamic-update-slice_fusion.2, f32[8,5,16,128]{3,2,0,1:T(8,128)S(1)} %broadcast_multiply_fusion), kind=kOutput, calls=%fused_computation.21 | convolution fusion | flops 75546624 | bytes 3735552 | tf_op jit(solution)/shard_map/iab,itbc->itac/dot_general | solution.py:35
  100.5 0.1 multiply_subtract_fusion
  100.6 0.7 copy.25
  (6 shorter events, 0.2 us)
Async XLA Ops:
  6.5 50.9 %all-gather.2.cloned.1.call-start = ((), (), s32[]{:S(2)}) async-start(), calls=%async_computation | async-start | bytes 2949120 | tf_op jit(solution)/shard_map/all_gather | solution.py:44
  57.5 25.0 %copy-start = (f32[8,5,128,128]{3,2,0,1:T(8,128)S(1)}, f32[8,5,128,128]{3,2,0,1:T(8,128)}, u32[]{:S(2)}) copy-start(f32[8,5,128,128]{3,2,0,1:T(8,128)} %all-gather.2.cloned.1.call-done) | copy-start | bytes 7864324
  59.0 23.4 %collective-permute-start = (f32[2,5,128,128]{3,2,0,1:T(8,128)S(1)}, f32[2,5,128,128]{3,2,0,1:T(8,128)S(1)}, u32[]{:S(2)}, u32[]{:S(2)}) collective-permute-start(f32[2,5,128,128]{3,2,0,1:T(8,128)S(1)} %get-tuple-element.142), channel_id=1, source_target_pairs={{0,1},{1,2},{2,3},{3,32},{32,33},{33,34},{34,35},{35,64},{64,65},{... | collective-permute-start | bytes 1966088 | tf_op jit(solution)/shard_map/ppermute | solution.py:17
  62.1 26.3 %collective-permute-start.1 = (f32[2,5,128,128]{3,2,0,1:T(8,128)S(1)}, f32[2,5,128,128]{3,2,0,1:T(8,128)S(1)}, u32[]{:S(2)}, u32[]{:S(2)}) collective-permute-start(f32[2,5,128,128]{3,2,0,1:T(8,128)S(1)} %get-tuple-element.141), channel_id=1, source_target_pairs={{1,0},{2,1},{3,2},{32,3},{33,32},{34,33},{35,34},{64,35},{65,64},{... | collective-permute-start | bytes 1966088 | tf_op jit(solution)/shard_map/ppermute | solution.py:19
  82.5 1.0 copy-start.1
Sparse Core Ops, SparseCore 0:
  9.4 47.9 all-gather.1
where the time goes:
time: 108 us
  waiting for transfers between devices  61.7 us (57%)
  matrix products  16.7 us (15%)
  between operations  13.5 us (12%)
  starting transfers between devices  10 us (9%)
  local copies, waits for them, and re-layouts  3.51 us (3%)
  other arithmetic  2.73 us (3%)
    all_gather x1, waiting for transfers between devices, shards(): whole_tiles = lax.all_gather(masked, 'col', axis=2, tiled=True)  48.3 us
    dot_general x10, matrix products, banded_local(): jnp.einsum('iab,itbc->itac', left_tiles[:, source], partner, precision=la...  16.7 us
    ppermute x1, waiting for transfers between devices, with_halo(): lax.ppermute(tail, axis, [(i, (i + 1) % count) for i in range(count)])  13.3 us
    ppermute x1, starting transfers between devices, with_halo(): lax.ppermute(head, axis, [((i + 1) % count, i) for i in range(count)])  6.94 us
    ppermute x1, starting transfers between devices, with_halo(): lax.ppermute(tail, axis, [(i, (i + 1) % count) for i in range(count)])  3.1 us
  transfers between devices with their start and end apart: 3, of which 2 were waited for; matrix products, arithmetic and copies ran while one was open for 5% of the time, Pallas kernels for 0%

commit v1 on v0

--- a/solution.py
+++ b/solution.py
@@ -5,6 +5,25 @@
 
 HALF = 2
 WIDE = 5
+
+
+def collect(x, axis, dim):
+    size, index, rows = (lax.axis_size(axis), lax.axis_index(axis), x.shape[dim])
+    right = [(i, (i + 1) % size) for i in range(size)]
+    left = [(i, (i - 1) % size) for i in range(size)]
+    out = jnp.zeros((*x.shape[:dim], size * rows, *x.shape[dim + 1 :]), x.dtype)
+    out = lax.dynamic_update_slice_in_dim(out, x, index * rows, axis=dim)
+    from_left = from_right = x
+    halfway = size // 2
+    for hop in range(1, halfway + 1):
+        from_left = lax.ppermute(from_left, axis, right)
+        out = lax.dynamic_update_slice_in_dim(out, from_left, (index - hop) % size * rows, axis=dim)
+        if hop < size - halfway:
+            from_right = lax.ppermute(from_right, axis, left)
+            out = lax.dynamic_update_slice_in_dim(
+                out, from_right, (index + hop) % size * rows, axis=dim
+            )
+    return out
 
 
 def with_halo(cells, sides, width):
@@ -41,7 +60,7 @@
 
 def shards(density, pattern):
     masked = density * pattern[:, :, None, None].astype(jnp.float32)
-    whole_tiles = lax.all_gather(masked, "col", axis=2, tiled=True)
+    whole_tiles = collect(masked, "col", 2)
     extended = with_halo(whole_tiles, ((("row", "depth"), 0),), HALF)
     square = banded_local(masked, extended, pattern)
     cube = banded_local(square, extended, pattern)

time: 108 us -> 91.6 us (0.85)
  starting transfers between devices: 10 us -> 38.7 us
  waiting for transfers between devices: 61.7 us -> 34.5 us
  between operations: 13.5 us -> 0.39 us
  matrix products: 16.7 us -> 12.5 us
  local copies, waits for them, and re-layouts: 3.51 us -> 1.55 us
    all_gather x1 -> x0, waiting for transfers between devices: 48.3 us -> none  [shards(): whole_tiles = lax.all_gather(masked, 'col', axis=2, tiled=True)]
    ppermute x0 -> x7, starting transfers between devices: none -> 28.3 us  [the longest x3 17.7 us: collect(): from_right = lax.ppermute(from_right, axis, left)]
    ppermute x0 -> x7, waiting for transfers between devices: none -> 20 us  [the longest x4 20 us: collect(): from_left = lax.ppermute(from_left, axis, right)]
    dot_general x10, matrix products: 16.7 us -> 12.5 us  [banded_local(): jnp.einsum('iab,itbc->itac', left_tiles[:, source], partner, precision=la...]
    slice x1, local copies, waits for them, and re-layouts: 1.53 us -> 0.13 us  [with_halo(): head = lax.slice_in_dim(cells, 0, width, axis=dim)]
    ppermute x1, waiting for transfers between devices: 0.01 us -> 1.18 us  [with_halo(): lax.ppermute(head, axis, [((i + 1) % count, i) for i in range(count)])]
  transfers between devices with their start and end apart: 3 -> 9, of which waited for: 2 -> 6; matrix products, arithmetic and copies ran while one was open for 5% -> 1% of each run, Pallas kernels for 0% -> 0%
where the time goes in v1:
time: 91.6 us; the launch traced here: 90.7 us
  starting transfers between devices  38.7 us (42%)
  waiting for transfers between devices  34.5 us (38%)
  matrix products  12.5 us (14%)
  other arithmetic  3.08 us (3%)
  local copies, waits for them, and re-layouts  1.55 us (2%)
    ppermute x4, waiting for transfers between devices, collect(): from_left = lax.ppermute(from_left, axis, right)  20 us
    ppermute x3, starting transfers between devices, collect(): from_right = lax.ppermute(from_right, axis, left)  17.7 us
    ppermute x1, waiting for transfers between devices, with_halo(): lax.ppermute(tail, axis, [(i, (i + 1) % count) for i in range(count)])  13.3 us
    dot_general x10, matrix products, banded_local(): jnp.einsum('iab,itbc->itac', left_tiles[:, source], partner, precision=la...  12.5 us
    ppermute x4, starting transfers between devices, collect(): from_left = lax.ppermute(from_left, axis, right)  10.6 us
    ppermute x1, starting transfers between devices, with_halo(): lax.ppermute(head, axis, [((i + 1) % count, i) for i in range(count)])  7.29 us
    ppermute x1, starting transfers between devices, with_halo(): lax.ppermute(tail, axis, [(i, (i + 1) % count) for i in range(count)])  3.12 us
  transfers between devices with their start and end apart: 9, of which 6 were waited for; matrix products, arithmetic and copies ran while one was open for 1% of the time, Pallas kernels for 0%

profile of v1, /device:TPU:1, one launch (start us, length us, event | category | flops | bytes accessed | tf_op | source)
XLA Modules:
  0.0 90.7 jit_solution(5755533475365448967)
XLA Ops:
  0.0 0.0 copy-start
  0.0 0.7 convert_element_type.6
  0.7 0.1 copy.3
  0.8 1.1 %copy_multiply_fusion = f32[8,5,16,128]{3,2,0,1:T(8,128)S(1)} fusion(f32[8,5,16,128]{3,2,1,0:T(8,128)} %param.26, f32[8,5]{0,1:T(8,128)S(1)} %copy.3), kind=kLoop, calls=%fused_computation.46 | loop fusion | flops 81920 | bytes 655520 | tf_op jit(solution)/shard_map/mul | solution.py:62
  1.9 4.8 %collective-permute-start = (f32[8,5,16,128]{3,2,0,1:T(8,128)S(1)}, f32[8,5,16,128]{3,2,0,1:T(8,128)S(1)}, u32[]{:S(2)}, u32[]{:S(2)}) collective-permute-start(f32[8,5,16,128]{3,2,0,1:T(8,128)S(1)} %copy_multiply_fusion), channel_id=1, source_target_pairs={{0,4},{4,8},{8,12},{12,16},{16,20},{20,24},{24,28},{28,0},{1,5},{5... | collective-permute-start | bytes 983048 | tf_op jit(solution)/shard_map/ppermute | solution.py:19
  6.7 8.6 %collective-permute-start.1 = (f32[8,5,16,128]{3,2,0,1:T(8,128)S(1)}, f32[8,5,16,128]{3,2,0,1:T(8,128)S(1)}, u32[]{:S(2)}, u32[]{:S(2)}) collective-permute-start(f32[8,5,16,128]{3,2,0,1:T(8,128)S(1)} %copy_multiply_fusion), channel_id=1, source_target_pairs={{0,28},{4,0},{8,4},{12,8},{16,12},{20,16},{24,20},{28,24},{1,29},{... | collective-permute-start | bytes 983048 | tf_op jit(solution)/shard_map/ppermute | solution.py:22
  15.5 0.3 broadcast_in_dim.2
  15.8 0.0 copy-done
  15.8 0.1 copy_dynamic-update-slice_fusion.7
  15.9 4.9 %collective-permute-done = f32[8,5,16,128]{3,2,0,1:T(8,128)S(1)} collective-permute-done((f32[8,5,16,128]{3,2,0,1:T(8,128)S(1)}, f32[8,5,16,128]{3,2,0,1:T(8,128)S(1)}, u32[]{:S(2)}, u32[]{:S(2)}) %collective-permute-start) | collective-permute-done | bytes 327712 | tf_op jit(solution)/shard_map/ppermute | solution.py:19
  20.8 1.9 %collective-permute-start.2 = (f32[8,5,16,128]{3,2,0,1:T(8,128)S(1)}, f32[8,5,16,128]{3,2,0,1:T(8,128)S(1)}, u32[]{:S(2)}, u32[]{:S(2)}) collective-permute-start(f32[8,5,16,128]{3,2,0,1:T(8,128)S(1)} %collective-permute-done), channel_id=1, source_target_pairs={{0,4},{4,8},{8,12},{12,16},{16,20},{20,24},{24,28},{28,0},{1,5},{5... | collective-permute-start | bytes 983048 | tf_op jit(solution)/shard_map/ppermute | solution.py:19
  22.7 0.0 collective-permute-done.1
  22.8 4.6 %collective-permute-start.3 = (f32[8,5,16,128]{3,2,0,1:T(8,128)S(1)}, f32[8,5,16,128]{3,2,0,1:T(8,128)S(1)}, u32[]{:S(2)}, u32[]{:S(2)}) collective-permute-start(f32[8,5,16,128]{3,2,0,1:T(8,128)S(1)} %collective-permute-done.1), channel_id=1, source_target_pairs={{0,28},{4,0},{8,4},{12,8},{16,12},{20,16},{24,20},{28,24},{1,29},{... | collective-permute-start | bytes 983048 | tf_op jit(solution)/shard_map/ppermute | solution.py:22
  27.4 4.5 %collective-permute-done.2 = f32[8,5,16,128]{3,2,0,1:T(8,128)S(1)} collective-permute-done((f32[8,5,16,128]{3,2,0,1:T(8,128)S(1)}, f32[8,5,16,128]{3,2,0,1:T(8,128)S(1)}, u32[]{:S(2)}, u32[]{:S(2)}) %collective-permute-start.2) | collective-permute-done | bytes 327712 | tf_op jit(solution)/shard_map/ppermute | solution.py:19
  31.9 1.9 %collective-permute-start.4 = (f32[8,5,16,128]{3,2,0,1:T(8,128)S(1)}, f32[8,5,16,128]{3,2,0,1:T(8,128)S(1)}, u32[]{:S(2)}, u32[]{:S(2)}) collective-permute-start(f32[8,5,16,128]{3,2,0,1:T(8,128)S(1)} %collective-permute-done.2), channel_id=1, source_target_pairs={{0,4},{4,8},{8,12},{12,16},{16,20},{20,24},{24,28},{28,0},{1,5},{5... | collective-permute-start | bytes 983048 | tf_op jit(solution)/shard_map/ppermute | solution.py:19
  33.8 0.0 collective-permute-done.3
  33.8 4.6 %collective-permute-start.5 = (f32[8,5,16,128]{3,2,0,1:T(8,128)S(1)}, f32[8,5,16,128]{3,2,0,1:T(8,128)S(1)}, u32[]{:S(2)}, u32[]{:S(2)}) collective-permute-start(f32[8,5,16,128]{3,2,0,1:T(8,128)S(1)} %collective-permute-done.3), channel_id=1, source_target_pairs={{0,28},{4,0},{8,4},{12,8},{16,12},{20,16},{24,20},{28,24},{1,29},{... | collective-permute-start | bytes 983048 | tf_op jit(solution)/shard_map/ppermute | solution.py:22
  38.5 3.5 %collective-permute-done.4 = f32[8,5,16,128]{3,2,0,1:T(8,128)S(1)} collective-permute-done((f32[8,5,16,128]{3,2,0,1:T(8,128)S(1)}, f32[8,5,16,128]{3,2,0,1:T(8,128)S(1)}, u32[]{:S(2)}, u32[]{:S(2)}) %collective-permute-start.4) | collective-permute-done | bytes 327712 | tf_op jit(solution)/shard_map/ppermute | solution.py:19
  42.0 1.9 %collective-permute-start.6 = (f32[8,5,16,128]{3,2,0,1:T(8,128)S(1)}, f32[8,5,16,128]{3,2,0,1:T(8,128)S(1)}, u32[]{:S(2)}, u32[]{:S(2)}) collective-permute-start(f32[8,5,16,128]{3,2,0,1:T(8,128)S(1)} %collective-permute-done.4), channel_id=1, source_target_pairs={{0,4},{4,8},{8,12},{12,16},{16,20},{20,24},{24,28},{28,0},{1,5},{5... | collective-permute-start | bytes 983048 | tf_op jit(solution)/shard_map/ppermute | solution.py:19
  44.0 0.0 collective-permute-done.5
  44.1 7.0 %collective-permute-done.6 = f32[8,5,16,128]{3,2,0,1:T(8,128)S(1)} collective-permute-done((f32[8,5,16,128]{3,2,0,1:T(8,128)S(1)}, f32[8,5,16,128]{3,2,0,1:T(8,128)S(1)}, u32[]{:S(2)}, u32[]{:S(2)}) %collective-permute-start.6) | collective-permute-done | bytes 327712 | tf_op jit(solution)/shard_map/ppermute | solution.py:19
  51.1 0.1 fusion.71
  51.2 3.1 %collective-permute-start.7 = (f32[2,5,128,128]{3,2,1,0:T(8,128)S(1)}, f32[2,5,128,128]{3,2,1,0:T(8,128)S(1)}, u32[]{:S(2)}, u32[]{:S(2)}) collective-permute-start(f32[2,5,128,128]{3,2,1,0:T(8,128)S(1)} %get-tuple-element.146), channel_id=1, source_target_pairs={{0,1},{1,2},{2,3},{3,32},{32,33},{33,34},{34,35},{35,64},{64,65},{... | collective-permute-start | bytes 1966088 | tf_op jit(solution)/shard_map/ppermute | solution.py:36
  54.4 7.3 %collective-permute-start.8 = (f32[2,5,128,128]{3,2,1,0:T(8,128)S(1)}, f32[2,5,128,128]{3,2,1,0:T(8,128)S(1)}, u32[]{:S(2)}, u32[]{:S(2)}) collective-permute-start(f32[2,5,128,128]{3,2,1,0:T(8,128)S(1)} %get-tuple-element.145), channel_id=1, source_target_pairs={{1,0},{2,1},{3,2},{32,3},{33,32},{34,33},{35,34},{64,35},{65,64},{... | collective-permute-start | bytes 1966088 | tf_op jit(solution)/shard_map/ppermute | solution.py:38
  61.7 13.3 %collective-permute-done.7 = f32[2,5,128,128]{3,2,1,0:T(8,128)S(1)} collective-permute-done((f32[2,5,128,128]{3,2,1,0:T(8,128)S(1)}, f32[2,5,128,128]{3,2,1,0:T(8,128)S(1)}, u32[]{:S(2)}, u32[]{:S(2)}) %collective-permute-start.7) | collective-permute-done | bytes 655392 | tf_op jit(solution)/shard_map/ppermute | solution.py:36
  75.0 1.2 %collective-permute-done.8 = f32[2,5,128,128]{3,2,1,0:T(8,128)S(1)} collective-permute-done((f32[2,5,128,128]{3,2,1,0:T(8,128)S(1)}, f32[2,5,128,128]{3,2,1,0:T(8,128)S(1)}, u32[]{:S(2)}, u32[]{:S(2)}) %collective-permute-start.8) | collective-permute-done | bytes 655392 | tf_op jit(solution)/shard_map/ppermute | solution.py:38
  76.2 0.4 pad_maximum_fusion.1
  76.6 1.1 %fusion.45 = f32[8,3,16,128]{3,2,0,1:T(8,128)S(1)} fusion(f32[8,3,128,128]{3,2,1,0:T(8,128)S(1)} %get-tuple-element.142, f32[8,5,16,128]{3,2,0,1:T(8,128)S(1)} %copy_multiply_fusion), kind=kOutput, calls=%fused_computation.34 | convolution fusion | flops 75497472 | bytes 1835008 | tf_op jit(solution)/shard_map/iab,itbc->itac/dot_general | solution.py:54
  77.8 0.5 fusion.4
  78.3 1.2 %add_dynamic-update-slice_fusion.1 = f32[8,5,16,128]{3,2,0,1:T(8,128)S(1)} fusion(f32[8,5,16,128]{3,2,0,1:T(8,128)S(1)} %scatter-add.26, f32[8,5,16,128]{3,2,0,1:T(8,128)S(1)} %copy_multiply_fusion, f32[8,4,128,128]{3,2,1,0:T(8,128)S(1)} %get-tuple-element.144), kind=kOutput, calls=%fused_computation.51 | convolution fusion | flops 100728832 | bytes 2686976 | tf_op jit(solution)/shard_map/iab,itbc->itac/dot_general | solution.py:54
  79.5 1.7 %fusion.24 = f32[8,5,16,128]{3,2,0,1:T(8,128)S(1)} fusion(f32[8,5,16,128]{3,2,0,1:T(8,128)S(1)} %add_dynamic-update-slice_fusion.1, f32[8,5,128,128]{3,2,1,0:T(8,128)S(1)} %copy_dynamic-update-slice_fusion, f32[8,5,16,128]{3,2,0,1:T(8,128)S(1)} %copy_multiply_fusion), kind=kOutput, calls=%fused_computation.27 | convolution fusion | flops 125911040 | bytes 3342336 | tf_op jit(solution)/shard_map/iab,itbc->itac/dot_general | solution.py:54
  81.1 1.2 %constant_dynamic-update-slice_fusion.1 = (f32[8,5,16,128]{3,2,0,1:T(8,128)S(1)}, f32[8,4,16,128]{3,2,0,1:T(8,128)S(1)}) fusion(f32[8,5,16,128]{3,2,0,1:T(8,128)S(1)} %fusion.24, f32[8,5,16,128]{3,2,0,1:T(8,128)S(1)} %copy_multiply_fusion, f32[8,4,128,128]{3,2,1,0:T(8,128)S(1)} %get-tuple-element.143), kind=kOutput, calls=%fused_computation.68 | convolution fusion | flops 100728832 | bytes 2949120 | tf_op jit(solution)/shard_map/iab,itbc->itac/dot_general | solution.py:54
  82.3 1.1 %fusion.58 = f32[8,5,16,128]{3,2,0,1:T(8,128)S(1)} fusion(f32[8,5,16,128]{3,2,0,1:T(8,128)S(1)} %get-tuple-element.147, f32[8,4,16,128]{3,2,0,1:T(8,128)S(1)} %get-tuple-element.148, f32[8,5,16,128]{3,2,0,1:T(8,128)S(1)} %copy_multiply_fusion, f32[8,3,128,128]{3,2,1,0:T(8,128)S(1)} %get-tuple-element.141), kind=kOutput, calls=%fused_computation.55 | convolution fusion | flops 75546624 | bytes 2031616 | tf_op jit(solution)/shard_map/iab,itbc->itac/dot_general | solution.py:54
  83.4 0.1 broadcast_multiply_fusion
  83.6 1.1 %fusion.48 = f32[8,3,16,128]{3,2,0,1:T(8,128)S(1)} fusion(f32[8,3,128,128]{3,2,1,0:T(8,128)S(1)} %get-tuple-element.142, f32[8,5,16,128]{3,2,0,1:T(8,128)S(1)} %broadcast_multiply_fusion), kind=kOutput, calls=%fused_computation.35 | convolution fusion | flops 75497472 | bytes 1835008 | tf_op jit(solution)/shard_map/iab,itbc->itac/dot_general | solution.py:54
  84.7 1.2 %add_dynamic-update-slice_fusion = f32[8,5,16,128]{3,2,0,1:T(8,128)S(1)} fusion(f32[8,5,16,128]{3,2,0,1:T(8,128)S(1)} %scatter-add.34, f32[8,5,16,128]{3,2,0,1:T(8,128)S(1)} %broadcast_multiply_fusion, f32[8,4,128,128]{3,2,1,0:T(8,128)S(1)} %get-tuple-element.144), kind=kOutput, calls=%fused_computation.50 | convolution fusion | flops 100728832 | bytes 2686976 | tf_op jit(solution)/shard_map/iab,itbc->itac/dot_general | solution.py:54
  85.9 1.7 %fusion.30 = f32[8,5,16,128]{3,2,0,1:T(8,128)S(1)} fusion(f32[8,5,16,128]{3,2,0,1:T(8,128)S(1)} %add_dynamic-update-slice_fusion, f32[8,5,128,128]{3,2,1,0:T(8,128)S(1)} %copy_dynamic-update-slice_fusion, f32[8,5,16,128]{3,2,0,1:T(8,128)S(1)} %broadcast_multiply_fusion), kind=kOutput, calls=%fused_computation.29 | convolution fusion | flops 125911040 | bytes 3342336 | tf_op jit(solution)/shard_map/iab,itbc->itac/dot_general | solution.py:54
  87.6 1.2 %constant_dynamic-update-slice_fusion = (f32[8,5,16,128]{3,2,0,1:T(8,128)S(1)}, f32[8,4,16,128]{3,2,0,1:T(8,128)S(1)}) fusion(f32[8,5,16,128]{3,2,0,1:T(8,128)S(1)} %fusion.30, f32[8,5,16,128]{3,2,0,1:T(8,128)S(1)} %broadcast_multiply_fusion, f32[8,4,128,128]{3,2,1,0:T(8,128)S(1)} %get-tuple-element.143), kind=kOutput, calls=%fused_computation.67 | convolution fusion | flops 100728832 | bytes 2949120 | tf_op jit(solution)/shard_map/iab,itbc->itac/dot_general | solution.py:54
  88.8 1.1 %fusion.57 = f32[8,5,16,128]{3,2,0,1:T(8,128)S(1)} fusion(f32[8,5,16,128]{3,2,0,1:T(8,128)S(1)} %get-tuple-element.149, f32[8,4,16,128]{3,2,0,1:T(8,128)S(1)} %get-tuple-element.150, f32[8,5,16,128]{3,2,0,1:T(8,128)S(1)} %broadcast_multiply_fusion, f32[8,3,128,128]{3,2,1,0:T(8,128)S(1)} %get-tuple-element.141), kind=kOutput, calls=%fused_computation.53 | convolution fusion | flops 75546624 | bytes 2031616 | tf_op jit(solution)/shard_map/iab,itbc->itac/dot_general | solution.py:54
  89.9 0.1 multiply_subtract_fusion
  90.0 0.7 copy.23
  (9 shorter events, 0.3 us)
Async XLA Ops:
  0.0 15.8 %copy-start = (f32[8,5,16,128]{3,2,1,0:T(8,128)S(1)}, f32[8,5,16,128]{3,2,1,0:T(8,128)}, u32[]{:S(2)}) copy-start(f32[8,5,16,128]{3,2,1,0:T(8,128)} %param.26) | copy-start | bytes 983044
  1.9 18.9 %collective-permute-start = (f32[8,5,16,128]{3,2,0,1:T(8,128)S(1)}, f32[8,5,16,128]{3,2,0,1:T(8,128)S(1)}, u32[]{:S(2)}, u32[]{:S(2)}) collective-permute-start(f32[8,5,16,128]{3,2,0,1:T(8,128)S(1)} %copy_multiply_fusion), channel_id=1, source_target_pairs={{0,4},{4,8},{8,12},{12,16},{16,20},{20,24},{24,28},{28,0},{1,5},{5... | collective-permute-start | bytes 983048 | tf_op jit(solution)/shard_map/ppermute | solution.py:19
  6.7 16.0 %collective-permute-start.1 = (f32[8,5,16,128]{3,2,0,1:T(8,128)S(1)}, f32[8,5,16,128]{3,2,0,1:T(8,128)S(1)}, u32[]{:S(2)}, u32[]{:S(2)}) collective-permute-start(f32[8,5,16,128]{3,2,0,1:T(8,128)S(1)} %copy_multiply_fusion), channel_id=1, source_target_pairs={{0,28},{4,0},{8,4},{12,8},{16,12},{20,16},{24,20},{28,24},{1,29},{... | collective-permute-start | bytes 983048 | tf_op jit(solution)/shard_map/ppermute | solution.py:22
  20.8 11.1 %collective-permute-start.2 = (f32[8,5,16,128]{3,2,0,1:T(8,128)S(1)}, f32[8,5,16,128]{3,2,0,1:T(8,128)S(1)}, u32[]{:S(2)}, u32[]{:S(2)}) collective-permute-start(f32[8,5,16,128]{3,2,0,1:T(8,128)S(1)} %collective-permute-done), channel_id=1, source_target_pairs={{0,4},{4,8},{8,12},{12,16},{16,20},{20,24},{24,28},{28,0},{1,5},{5... | collective-permute-start | bytes 983048 | tf_op jit(solution)/shard_map/ppermute | solution.py:19
  22.8 11.1 %collective-permute-start.3 = (f32[8,5,16,128]{3,2,0,1:T(8,128)S(1)}, f32[8,5,16,128]{3,2,0,1:T(8,128)S(1)}, u32[]{:S(2)}, u32[]{:S(2)}) collective-permute-start(f32[8,5,16,128]{3,2,0,1:T(8,128)S(1)} %collective-permute-done.1), channel_id=1, source_target_pairs={{0,28},{4,0},{8,4},{12,8},{16,12},{20,16},{24,20},{28,24},{1,29},{... | collective-permute-start | bytes 983048 | tf_op jit(solution)/shard_map/ppermute | solution.py:22
  31.9 10.1 %collective-permute-start.4 = (f32[8,5,16,128]{3,2,0,1:T(8,128)S(1)}, f32[8,5,16,128]{3,2,0,1:T(8,128)S(1)}, u32[]{:S(2)}, u32[]{:S(2)}) collective-permute-start(f32[8,5,16,128]{3,2,0,1:T(8,128)S(1)} %collective-permute-done.2), channel_id=1, source_target_pairs={{0,4},{4,8},{8,12},{12,16},{16,20},{20,24},{24,28},{28,0},{1,5},{5... | collective-permute-start | bytes 983048 | tf_op jit(solution)/shard_map/ppermute | solution.py:19
  33.8 10.2 %collective-permute-start.5 = (f32[8,5,16,128]{3,2,0,1:T(8,128)S(1)}, f32[8,5,16,128]{3,2,0,1:T(8,128)S(1)}, u32[]{:S(2)}, u32[]{:S(2)}) collective-permute-start(f32[8,5,16,128]{3,2,0,1:T(8,128)S(1)} %collective-permute-done.3), channel_id=1, source_target_pairs={{0,28},{4,0},{8,4},{12,8},{16,12},{20,16},{24,20},{28,24},{1,29},{... | collective-permute-start | bytes 983048 | tf_op jit(solution)/shard_map/ppermute | solution.py:22
  42.0 9.0 %collective-permute-start.6 = (f32[8,5,16,128]{3,2,0,1:T(8,128)S(1)}, f32[8,5,16,128]{3,2,0,1:T(8,128)S(1)}, u32[]{:S(2)}, u32[]{:S(2)}) collective-permute-start(f32[8,5,16,128]{3,2,0,1:T(8,128)S(1)} %collective-permute-done.4), channel_id=1, source_target_pairs={{0,4},{4,8},{8,12},{12,16},{16,20},{20,24},{24,28},{28,0},{1,5},{5... | collective-permute-start | bytes 983048 | tf_op jit(solution)/shard_map/ppermute | solution.py:19
  51.2 23.8 %collective-permute-start.7 = (f32[2,5,128,128]{3,2,1,0:T(8,128)S(1)}, f32[2,5,128,128]{3,2,1,0:T(8,128)S(1)}, u32[]{:S(2)}, u32[]{:S(2)}) collective-permute-start(f32[2,5,128,128]{3,2,1,0:T(8,128)S(1)} %get-tuple-element.146), channel_id=1, source_target_pairs={{0,1},{1,2},{2,3},{3,32},{32,33},{33,34},{34,35},{35,64},{64,65},{... | collective-permute-start | bytes 1966088 | tf_op jit(solution)/shard_map/ppermute | solution.py:36
  54.4 21.8 %collective-permute-start.8 = (f32[2,5,128,128]{3,2,1,0:T(8,128)S(1)}, f32[2,5,128,128]{3,2,1,0:T(8,128)S(1)}, u32[]{:S(2)}, u32[]{:S(2)}) collective-permute-start(f32[2,5,128,128]{3,2,1,0:T(8,128)S(1)} %get-tuple-element.145), channel_id=1, source_target_pairs={{1,0},{2,1},{3,2},{32,3},{33,32},{34,33},{35,34},{64,35},{65,64},{... | collective-permute-start | bytes 1966088 | tf_op jit(solution)/shard_map/ppermute | solution.py:38
